TPU v7x, 128 devices: a whole 4x4x4 slice. The times are simulated.
128 devices in a mesh: dp: 32 (over z, y_hi, x), row: 2 (over core), col: 2 (over y_lo).
Axes of the slice: x: 4, y: 4 (y_hi: 2, y_lo: 2; y = y_hi * 2 + y_lo), z: 4, core: 2. Of those that a mesh axis runs over, the one named last changes fastest.
Arguments:
- hidden_in: bfloat16 [32768, 1536], P(('dp', 'row'), 'col'), may hold values from -64 to 64
- gain_attn: float32 [1536], P('col'), may hold values from 0.25 to 3.5
- w_query: bfloat16 [1536, 1536], P('col', 'row'), may hold values from -0.21875 to 0.21875
- w_key: bfloat16 [1536, 768], P('col', 'row'), may hold values from -0.21875 to 0.21875
- w_value: bfloat16 [1536, 768], P('col', 'row'), may hold values from -0.15625 to 0.15625
- w_out: bfloat16 [1536, 1536], P('row', 'col'), may hold values from -0.4375 to 0.4375
- gain_mlp: float32 [1536], P('col'), may hold values from 0.25 to 3.5
- w_gate: bfloat16 [1536, 4096], P('col', 'row'), may hold values from -0.15625 to 0.15625
- w_up: bfloat16 [1536, 4096], P('col', 'row'), may hold values from -0.15625 to 0.15625
- w_down: bfloat16 [4096, 1536], P('row', 'col'), may hold values from -0.1875 to 0.1875
- out_grad: bfloat16 [32768, 1536], P(('dp', 'row'), 'col'), may hold values from -42 to 42
Outputs:
- block_out: bfloat16 [32768, 1536], P(('dp', 'row'), 'col')
- in_grad: bfloat16 [32768, 1536], P(('dp', 'row'), 'col')
- grad_gain_attn: float32 [1536], P('col')
- grad_w_query: float32 [1536, 1536], P('col', 'row')
- grad_w_key: float32 [1536, 768], P('col', 'row')
- grad_w_value: float32 [1536, 768], P('col', 'row')
- grad_w_out: float32 [1536, 1536], P('row', 'col')
- grad_gain_mlp: float32 [1536], P('col')
- grad_w_gate: float32 [1536, 4096], P('col', 'row')
- grad_w_up: float32 [1536, 4096], P('col', 'row')
- grad_w_down: float32 [4096, 1536], P('row', 'col')
All inputs are finite; a program needn't handle non-finite values.
Results may differ from a plain program's by a relative error of at most 0.03.
Values may be sent and summed in bfloat16 or wider, within the bound.
A program may use at most 256 MiB of HBM per device.

v0:
```python
import math

import jax
import jax.numpy as jnp
from jax import lax
from jax.sharding import PartitionSpec as P

HEAD_DIM = 96


EPS = 1e-05
ROPE_BASE = 100000.0
NEG = -1e30


def matmul(left, right):
    return jnp.dot(left, right, preferred_element_type=jnp.float32)


def inner_left(left, right):
    return lax.dot_general(
        left, right, (((0,), (0,)), ((), ())), preferred_element_type=jnp.float32
    )


def inner_right(left, right):
    return lax.dot_general(
        left, right, (((1,), (1,)), ((), ())), preferred_element_type=jnp.float32
    )


def rotary(length):
    half = HEAD_DIM // 2
    rates = jnp.exp(-math.log(ROPE_BASE) * 2.0 * jnp.arange(half, dtype=jnp.float32) / HEAD_DIM)
    angle = jnp.arange(length, dtype=jnp.float32)[:, None] * rates[None, :]
    return (jnp.cos(angle)[:, None, :], jnp.sin(angle)[:, None, :])


def rotate(value, cosine, sine):
    half = value.shape[-1] // 2
    first = value[..., :half]
    second = value[..., half:]
    return jnp.concatenate(
        [first * cosine - second * sine, second * cosine + first * sine], axis=-1
    )


def rotate_back(grad, cosine, sine):
    half = grad.shape[-1] // 2
    first = grad[..., :half]
    second = grad[..., half:]
    return jnp.concatenate(
        [first * cosine + second * sine, second * cosine - first * sine], axis=-1
    )


def norm_forward(resid, gain):
    width = resid.shape[1] * lax.axis_size("col")
    squares = lax.psum(jnp.sum(resid * resid, axis=1), "col")
    factor = lax.rsqrt(squares / width + EPS)[:, None]
    normed = resid * factor
    return (normed, factor, (normed * gain).astype(jnp.bfloat16))


def norm_backward(grad_scaled, normed, factor, gain):
    width = normed.shape[1] * lax.axis_size("col")
    grad_normed = grad_scaled * gain
    projection = lax.psum(jnp.sum(grad_normed * normed, axis=1), "col")
    grad_resid = factor * (grad_normed - normed * (projection / width)[:, None])
    return (grad_resid, jnp.sum(grad_scaled * normed, axis=0))


def gather_tokens(value):
    return lax.all_gather(value, "row", axis=0, tiled=True)


def sum_heads(first, second):
    return (
        lax.psum_scatter(first, "col", scatter_dimension=1, tiled=True),
        lax.psum_scatter(second, "col", scatter_dimension=1, tiled=True),
    )


def gather_heads(value):
    return lax.all_gather(value, "col", axis=1, tiled=True)


def sum_tokens(gathered, weight, count_rows):

    def term(start, count):
        return matmul(gathered, weight)

    return lax.psum_scatter(
        term(jnp.int32(0), count_rows * lax.axis_size("row")),
        "row",
        scatter_dimension=0,
        tiled=True,
    )


def gather_tokens_back(value):
    return lax.all_gather(value, "row", axis=0, tiled=True)


def sum_heads_back(value):
    return lax.psum_scatter(value, "col", scatter_dimension=1, tiled=True)


def gather_heads_back(first, second):
    return (
        lax.all_gather(first, "col", axis=1, tiled=True),
        lax.all_gather(second, "col", axis=1, tiled=True),
    )


def sum_tokens_back(first, first_weight, second, second_weight, count_rows):

    def term(start, count):
        left = inner_right(first, first_weight)
        return left + inner_right(second, second_weight)

    return lax.psum_scatter(
        term(jnp.int32(0), count_rows * lax.axis_size("row")),
        "row",
        scatter_dimension=0,
        tiled=True,
    )


def attend(query, keys, values):
    length = query.shape[0]
    kv_heads = keys.shape[1]
    group = query.shape[1] // kv_heads
    block = min(512, length)
    scale = 1.0 / math.sqrt(HEAD_DIM)
    outputs = []
    log_totals = []
    for index in range(length // block):
        start = index * block
        reach = start + block
        piece = query[start:reach].reshape(block, kv_heads, group, HEAD_DIM)
        raw = jnp.einsum("qkgd,tkd->kgqt", piece, keys[:reach], preferred_element_type=jnp.float32)
        causal = jnp.arange(reach)[None, :] <= (start + jnp.arange(block))[:, None]
        scores = jnp.where(causal, raw * scale, NEG)
        top = jnp.max(scores, axis=-1, keepdims=True)
        powers = jnp.exp(scores - top)
        total = jnp.sum(powers, axis=-1, keepdims=True)
        shares = (powers / total).astype(jnp.bfloat16)
        mixed = jnp.einsum(
            "kgqt,tkd->qkgd", shares, values[:reach], preferred_element_type=jnp.float32
        )
        outputs.append(mixed.reshape(block, kv_heads * group * HEAD_DIM))
        log_totals.append(top + jnp.log(total))
    return (jnp.concatenate(outputs, axis=0), log_totals)


def attend_back(query, keys, values, grad_out, log_totals):
    length = query.shape[0]
    kv_heads = keys.shape[1]
    group = query.shape[1] // kv_heads
    block = min(512, length)
    scale = 1.0 / math.sqrt(HEAD_DIM)
    grad_queries = []
    grad_keys = jnp.zeros(keys.shape, jnp.float32)
    grad_values = jnp.zeros(values.shape, jnp.float32)
    for index in range(length // block):
        start = index * block
        reach = start + block
        piece = query[start:reach].reshape(block, kv_heads, group, HEAD_DIM)
        back = grad_out[start:reach].reshape(block, kv_heads, group, HEAD_DIM)
        raw = jnp.einsum("qkgd,tkd->kgqt", piece, keys[:reach], preferred_element_type=jnp.float32)
        causal = jnp.arange(reach)[None, :] <= (start + jnp.arange(block))[:, None]
        scores = jnp.where(causal, raw * scale, NEG)
        shares = jnp.exp(scores - log_totals[index])
        shares_low = shares.astype(jnp.bfloat16)
        grad_shares = jnp.einsum(
            "qkgd,tkd->kgqt", back, values[:reach], preferred_element_type=jnp.float32
        )
        center = jnp.sum(grad_shares * shares, axis=-1, keepdims=True)
        grad_raw = (shares * (grad_shares - center) * scale).astype(jnp.bfloat16)
        grad_piece = jnp.einsum(
            "kgqt,tkd->qkgd", grad_raw, keys[:reach], preferred_element_type=jnp.float32
        )
        grad_queries.append(grad_piece.reshape(block, kv_heads * group, HEAD_DIM))
        grad_keys = grad_keys.at[:reach].add(
            jnp.einsum("kgqt,qkgd->tkd", grad_raw, piece, preferred_element_type=jnp.float32)
        )
        grad_values = grad_values.at[:reach].add(
            jnp.einsum("kgqt,qkgd->tkd", shares_low, back, preferred_element_type=jnp.float32)
        )
    return (jnp.concatenate(grad_queries, axis=0), grad_keys, grad_values)


def per_device(
    hidden_in, gain_attn, w_query, w_key, w_value, w_out, gain_mlp, w_gate, w_up, w_down, out_grad
):
    count_rows = hidden_in.shape[0]
    col_count = lax.axis_size("col")
    key_width = w_key.shape[1] // col_count
    local_width = w_key.shape[0]
    w_keyval = jnp.stack(
        [
            w_key.reshape(local_width, col_count, key_width),
            w_value.reshape(local_width, col_count, key_width),
        ],
        axis=2,
    ).reshape(local_width, col_count * 2 * key_width)
    resid = hidden_in.astype(jnp.float32)
    normed_attn, factor_attn, scaled_attn = norm_forward(resid, gain_attn)
    gathered_attn = gather_tokens(scaled_attn)
    query_pre, keyval_pre = sum_heads(
        matmul(gathered_attn, w_query), matmul(gathered_attn, w_keyval)
    )
    length = gathered_attn.shape[0]
    cosine, sine = rotary(length)
    query_rot = rotate(query_pre.reshape(length, -1, HEAD_DIM), cosine, sine).astype(jnp.bfloat16)
    keys_rot = rotate(keyval_pre[:, :key_width].reshape(length, -1, HEAD_DIM), cosine, sine).astype(
        jnp.bfloat16
    )
    values = keyval_pre[:, key_width:].reshape(length, -1, HEAD_DIM).astype(jnp.bfloat16)
    attended, log_totals = attend(query_rot, keys_rot, values)
    heads_row = gather_heads(attended.astype(jnp.bfloat16))
    middle = resid + sum_tokens(heads_row, w_out, count_rows)
    normed_mlp, factor_mlp, scaled_mlp = norm_forward(middle, gain_mlp)
    gathered_mlp = gather_tokens(scaled_mlp)
    gate, upper = sum_heads(matmul(gathered_mlp, w_gate), matmul(gathered_mlp, w_up))
    logistic = jax.nn.sigmoid(gate)
    activated = gate * logistic
    hidden_row = gather_heads((activated * upper).astype(jnp.bfloat16))
    block_out = (middle + sum_tokens(hidden_row, w_down, count_rows)).astype(jnp.bfloat16)
    grad_rows_out = gather_tokens_back(out_grad)
    grad_w_down = inner_left(hidden_row, grad_rows_out)
    grad_hidden = sum_heads_back(inner_right(grad_rows_out, w_down))
    grad_gate = grad_hidden * upper * logistic * (1.0 + gate * (1.0 - logistic))
    grad_upper = grad_hidden * activated
    gate_rows, upper_rows = gather_heads_back(
        grad_gate.astype(jnp.bfloat16), grad_upper.astype(jnp.bfloat16)
    )
    grad_w_gate = inner_left(gathered_mlp, gate_rows)
    grad_w_up = inner_left(gathered_mlp, upper_rows)
    grad_scaled_mlp = sum_tokens_back(gate_rows, w_gate, upper_rows, w_up, count_rows)
    grad_middle_norm, gain_mlp_part = norm_backward(
        grad_scaled_mlp, normed_mlp, factor_mlp, gain_mlp
    )
    grad_middle = out_grad.astype(jnp.float32) + grad_middle_norm
    grad_middle_rows = gather_tokens_back(grad_middle.astype(jnp.bfloat16))
    grad_w_out = inner_left(heads_row, grad_middle_rows)
    grad_attended = sum_heads_back(inner_right(grad_middle_rows, w_out)).astype(jnp.bfloat16)
    grad_query, grad_keys, grad_values = attend_back(
        query_rot, keys_rot, values, grad_attended, log_totals
    )
    grad_query_pre = rotate_back(grad_query, cosine, sine).reshape(length, -1).astype(jnp.bfloat16)
    grad_key_pre = rotate_back(grad_keys, cosine, sine).reshape(length, -1)
    grad_keyval = jnp.concatenate([grad_key_pre, grad_values.reshape(length, -1)], axis=1).astype(
        jnp.bfloat16
    )
    query_rows, keyval_rows = gather_heads_back(grad_query_pre, grad_keyval)
    grad_w_query = inner_left(gathered_attn, query_rows)
    grad_w_keyval = inner_left(gathered_attn, keyval_rows).reshape(
        local_width, col_count, 2, key_width
    )
    grad_w_key = grad_w_keyval[:, :, 0, :].reshape(w_key.shape)
    grad_w_value = grad_w_keyval[:, :, 1, :].reshape(w_value.shape)
    grad_scaled_attn = sum_tokens_back(query_rows, w_query, keyval_rows, w_keyval, count_rows)
    grad_resid_norm, gain_attn_part = norm_backward(
        grad_scaled_attn, normed_attn, factor_attn, gain_attn
    )
    in_grad = (grad_middle + grad_resid_norm).astype(jnp.bfloat16)
    gain_attn_rows, gain_mlp_rows = lax.psum((gain_attn_part, gain_mlp_part), "row")
    summed = (
        lax.psum(grad_w_query.astype(jnp.bfloat16), "dp").astype(jnp.float32),
        lax.psum(grad_w_key.astype(jnp.bfloat16), "dp").astype(jnp.float32),
        lax.psum(grad_w_value.astype(jnp.bfloat16), "dp").astype(jnp.float32),
        lax.psum(grad_w_out.astype(jnp.bfloat16), "dp").astype(jnp.float32),
        lax.psum(grad_w_gate.astype(jnp.bfloat16), "dp").astype(jnp.float32),
        lax.psum(grad_w_up.astype(jnp.bfloat16), "dp").astype(jnp.float32),
        lax.psum(grad_w_down.astype(jnp.bfloat16), "dp").astype(jnp.float32),
        lax.psum(gain_attn_rows.astype(jnp.bfloat16), "dp").astype(jnp.float32),
        lax.psum(gain_mlp_rows.astype(jnp.bfloat16), "dp").astype(jnp.float32),
    )
    return (
        block_out,
        in_grad,
        summed[7],
        summed[0],
        summed[1],
        summed[2],
        summed[3],
        summed[8],
        summed[4],
        summed[5],
        summed[6],
    )


def solution(mesh):
    return jax.shard_map(
        per_device,
        mesh=mesh,
        in_specs=(
            P(("dp", "row"), "col"),
            P("col"),
            P("col", "row"),
            P("col", "row"),
            P("col", "row"),
            P("row", "col"),
            P("col"),
            P("col", "row"),
            P("col", "row"),
            P("row", "col"),
            P(("dp", "row"), "col"),
        ),
        out_specs=(
            P(("dp", "row"), "col"),
            P(("dp", "row"), "col"),
            P("col"),
            P("col", "row"),
            P("col", "row"),
            P("col", "row"),
            P("row", "col"),
            P("col"),
            P("col", "row"),
            P("col", "row"),
            P("row", "col"),
        ),
        check_vma=False,
    )
```

profile of v0, /device:TPU:0, one launch (start us, length us, event | category | flops | bytes accessed | tf_op | source)
XLA Modules:
  0.0 1440.5 jit_solution(8787200410320081369)
XLA Ops:
  23.3 8.4 all-gather.11.cloned.1.call-done
  44.5 39.4 %reduce-scatter.11.cloned.1.call-done = f32[1024,384]{1,0:T(8,128)} async-done(((f32[1024,768]{1,0:T(8,128)}), f32[1024,384]{1,0:T(8,128)}) %reduce-scatter.11.cloned.1.call-update) | async-done | bytes 1572880 | tf_op jit(solution)/shard_map/reduce_scatter | solution.py:80
  90.9 42.9 %reduce-scatter.13.cloned.1.call-done = f32[1024,384]{1,0:T(8,128)} async-done(((f32[1024,768]{1,0:T(8,128)}), f32[1024,384]{1,0:T(8,128)}) %reduce-scatter.13.cloned.1.call-update) | async-done | bytes 1572880 | tf_op jit(solution)/shard_map/reduce_scatter | solution.py:79
  158.5 30.8 %all-gather.13.cloned.1.call-done = bf16[1024,768]{0,1:T(8,128)(2,1)} async-done(((bf16[1024,384]{0,1:T(8,128)(2,1)}), bf16[1024,768]{0,1:T(8,128)(2,1)}) %all-gather.13.cloned.1.call-update) | async-done | bytes 1572880 | tf_op jit(solution)/shard_map/all_gather | solution.py:85
  194.8 14.0 reduce-scatter.15.cloned.1.call-done
  224.3 9.1 fusion.90
  233.5 7.1 all-gather.15.cloned.1.call-done
  240.5 9.1 fusion.88
  249.7 7.1 fusion.87
  256.9 89.3 %reduce-scatter.23.cloned.1.call-done = f32[1024,1024]{1,0:T(8,128)} async-done(((f32[1024,2048]{1,0:T(8,128)}), f32[1024,1024]{1,0:T(8,128)}) %reduce-scatter.23.cloned.1.call-update) | async-done | bytes 4194320 | tf_op jit(solution)/shard_map/reduce_scatter | solution.py:106
  346.2 105.2 %reduce-scatter.19.cloned.1.call-done = f32[1024,1024]{1,0:T(8,128)} async-done(((f32[1024,2048]{1,0:T(8,128)}), f32[1024,1024]{1,0:T(8,128)}) %reduce-scatter.19.cloned.1.call-update) | async-done | bytes 4194320 | tf_op jit(solution)/shard_map/reduce_scatter | solution.py:80
  451.4 105.1 %reduce-scatter.17.cloned.1.call-done = f32[1024,1024]{1,0:T(8,128)} async-done(((f32[1024,2048]{1,0:T(8,128)}), f32[1024,1024]{1,0:T(8,128)}) %reduce-scatter.17.cloned.1.call-update) | async-done | bytes 4194320 | tf_op jit(solution)/shard_map/reduce_scatter | solution.py:79
  556.6 8.4 multiply_convert_fusion
  566.2 59.2 %all-gather.21.cloned.1.call-done = bf16[1024,2048]{1,0:T(8,128)(2,1)} async-done(((bf16[1024,1024]{1,0:T(8,128)(2,1)}), bf16[1024,2048]{1,0:T(8,128)(2,1)}) %all-gather.21.cloned.1.call-update) | async-done | bytes 4194320 | tf_op jit(solution)/shard_map/all_gather | solution.py:111
  625.4 7.3 fusion.91
  632.7 55.1 %all-gather.23.cloned.1.call-done = bf16[1024,2048]{1,0:T(8,128)(2,1)} async-done(((bf16[1024,1024]{1,0:T(8,128)(2,1)}), bf16[1024,2048]{1,0:T(8,128)(2,1)}) %all-gather.23.cloned.1.call-update) | async-done | bytes 4194320 | tf_op jit(solution)/shard_map/all_gather | solution.py:112
  687.7 9.1 convolution_add_fusion.1
  697.0 14.6 %reduce-scatter.25.cloned.1.call-done = f32[512,768]{1,0:T(8,128)} async-done(((f32[1024,768]{1,0:T(8,128)}), f32[512,768]{1,0:T(8,128)}) %reduce-scatter.25.cloned.1.call-update) | async-done | bytes 1572880 | tf_op jit(solution)/shard_map/reduce_scatter | solution.py:122
  714.1 5.6 psum.107
  723.6 14.0 all-gather.25.cloned.1.call-done
  744.3 45.5 %reduce-scatter.27.cloned.1.call-done = f32[1024,384]{1,0:T(8,128)} async-done(((f32[1024,768]{1,0:T(8,128)}), f32[1024,384]{1,0:T(8,128)}) %reduce-scatter.27.cloned.1.call-update) | async-done | bytes 1572880 | tf_op jit(solution)/shard_map/reduce_scatter | solution.py:106
  795.3 8.7 fusion.52
  804.0 9.0 fusion.29
  817.7 15.6 %fusion.19 = f32[2,96,2,512]{3,1,2,0:T(8,128)} fusion(f32[2,1024,512,2]{2,1,3,0:T(8,128)} %fusion.94, f32[2,2,512,1024]{2,3,1,0:T(8,128)} %copy-done.3, f32[2,2,512]{2,1,0:T(2,128)} %log_add_fusion, bf16[1024,2,48]{0,2,1:T(8,128)(2,1)S(1)} %copy-done.26, bf16[1024,2,48]{0,2,1:T(8,128)(2,1)S(1)} %copy-done.24), kind=kOutput, calls=%fused_computation.37 | convolution fusion | flops 418122752 | bytes 17965056 | tf_op jit(solution)/shard_map/kgqt,tkd->qkgd/dot_general | solution.py:181
  836.4 15.3 %fusion.40 = f32[1024,2,96]{0,2,1:T(8,128)S(1)} fusion(bf16[512,2,2,96]{0,3,2,1:T(8,128)(2,1)} %bitcast.210, f32[2,1024,512,2]{2,1,3,0:T(8,128)} %fusion.94, f32[2,2,512,1024]{2,3,1,0:T(8,128)} %copy-done.3, f32[2,2,512]{2,1,0:T(2,128)} %log_add_fusion, f32[512,2,96]{0,2,1:T(8,128)} %fusion.52), kind=kOutput, calls=%fused_computation.74 | convolution fusion | flops 417532928 | bytes 18358272 | tf_op jit(solution)/shard_map/kgqt,qkgd->tkd/dot_general | solution.py:186
  861.3 5.7 all-gather.27.cloned.1.call-done
  871.9 28.0 %all-gather.29.cloned.1.call-done = bf16[1024,768]{0,1:T(8,128)(2,1)} async-done(((bf16[1024,384]{0,1:T(8,128)(2,1)}), bf16[1024,768]{0,1:T(8,128)(2,1)}) %all-gather.29.cloned.1.call-update) | async-done | bytes 1572880 | tf_op jit(solution)/shard_map/all_gather | solution.py:112
  905.4 56.8 %all-gather.17.cloned.1.call-done = bf16[1024,2048]{1,0:T(8,128)(2,1)} async-done(((bf16[1024,1024]{1,0:T(8,128)(2,1)}), bf16[1024,2048]{1,0:T(8,128)(2,1)}) %all-gather.17.cloned.1.call-update) | async-done | bytes 4194320 | tf_op jit(solution)/shard_map/all_gather | solution.py:85
  962.2 8.2 fusion.89
  971.9 7.5 convolution_convert_fusion
  1002.1 96.2 %all-reduce.3 = (bf16[768]{0:T(1024)(128)(2,1)S(1)}, bf16[768]{0:T(1024)(128)(2,1)S(1)}) all-reduce(bf16[768]{0:T(1024)(128)(2,1)S(1)} %get-tuple-element.90, bf16[768]{0:T(1024)(128)(2,1)S(1)} %get-tuple-element.91), channel_id=1, replica_groups=mesh['dp'=32,'row'=2,'col'=2] {'dp'}, use_global_device_ids=true, to_apply=%region_26.27 | all-reduce | flops 1536 | bytes 6144 | tf_op jit(solution)/shard_map/psum | solution.py:278
  1109.3 305.9 %all-reduce.7.cloned.1.call-done = (bf16[768,384]{0,1:T(8,128)(2,1)}, bf16[768,384]{0,1:T(8,128)(2,1)}, bf16[768,768]{1,0:T(8,128)(2,1)}, bf16[768,768]{1,0:T(8,...) async-done(((bf16[768,384]{0,1:T(8,128)(2,1)}, bf16[768,384]{0,1:T(8,128)(2,1)}, bf16[768,768]{1,0:T(8,128)(2,1)}, ...) | async-done | bytes 12976144 | tf_op jit(solution)/shard_map/psum | solution.py:272
  (226 shorter events, 182.4 us)
Async XLA Ops:
  7.2 242.5 %copy-start = (bf16[768,2048]{1,0:T(8,128)(2,1)S(1)}, bf16[768,2048]{1,0:T(8,128)(2,1)}, u32[]{:S(2)}) copy-start(bf16[768,2048]{1,0:T(8,128)(2,1)} %param.30) | copy-start | bytes 9437188
  7.2 24.5 %all-gather.11.cloned.1.call-start = ((), (), s32[]{:S(2)}) async-start(), calls=%async_computation.10 | async-start | bytes 2359296 | tf_op jit(solution)/shard_map/all_gather | solution.py:74
  16.6 67.3 %reduce-scatter.11.cloned.1.call-start = ((), (), s32[]{:S(2)}) async-start(), calls=%async_computation.11 | async-start | bytes 4718592 | tf_op jit(solution)/shard_map/reduce_scatter | solution.py:80
  36.5 97.3 %reduce-scatter.13.cloned.1.call-start = ((), (), s32[]{:S(2)}) async-start(), calls=%async_computation.12 | async-start | bytes 4718592 | tf_op jit(solution)/shard_map/reduce_scatter | solution.py:79
  41.4 147.9 %all-gather.13.cloned.1.call-start = ((), (), s32[]{:S(2)}) async-start(), calls=%async_computation.13 | async-start | bytes 2359296 | tf_op jit(solution)/shard_map/all_gather | solution.py:85
  158.4 50.4 %reduce-scatter.15.cloned.1.call-start = ((), (), s32[]{:S(2)}) async-start(), calls=%async_computation.14 | async-start | bytes 4718592 | tf_op jit(solution)/shard_map/reduce_scatter | solution.py:93
  194.2 23.8 %copy-start.27 = (f32[768]{0:T(1024)S(1)}, f32[768]{0:T(1024)}, u32[]{:S(2)}) copy-start(f32[768]{0:T(1024)} %param.29) | copy-start | bytes 9220
  194.2 30.2 %all-gather.19.cloned.1.call-start = ((), (), s32[]{:S(2)}) async-start(), calls=%async_computation.20 | async-start | bytes 2359296 | tf_op jit(solution)/shard_map/all_gather | solution.py:102
  194.8 45.8 %all-gather.15.cloned.1.call-start = ((), (), s32[]{:S(2)}) async-start(), calls=%async_computation.15 | async-start | bytes 2359296 | tf_op jit(solution)/shard_map/all_gather | solution.py:74
  220.5 125.7 %reduce-scatter.23.cloned.1.call-start = ((), (), s32[]{:S(2)}) async-start(), calls=%async_computation.21 | async-start | bytes 12582912 | tf_op jit(solution)/shard_map/reduce_scatter | solution.py:106
  233.4 218.0 %reduce-scatter.19.cloned.1.call-start = ((), (), s32[]{:S(2)}) async-start(), calls=%async_computation.17 | async-start | bytes 12582912 | tf_op jit(solution)/shard_map/reduce_scatter | solution.py:80
  249.6 306.9 %reduce-scatter.17.cloned.1.call-start = ((), (), s32[]{:S(2)}) async-start(), calls=%async_computation.16 | async-start | bytes 12582912 | tf_op jit(solution)/shard_map/reduce_scatter | solution.py:79
  256.8 368.5 %all-gather.21.cloned.1.call-start = ((), (), s32[]{:S(2)}) async-start(), calls=%async_computation.22 | async-start | bytes 6291456 | tf_op jit(solution)/shard_map/all_gather | solution.py:111
  565.0 122.8 %all-gather.23.cloned.1.call-start = ((), (), s32[]{:S(2)}) async-start(), calls=%async_computation.23 | async-start | bytes 6291456 | tf_op jit(solution)/shard_map/all_gather | solution.py:112
  565.5 146.0 %reduce-scatter.25.cloned.1.call-start = ((), (), s32[]{:S(2)}) async-start(), calls=%async_computation.24 | async-start | bytes 4718592 | tf_op jit(solution)/shard_map/reduce_scatter | solution.py:122
  696.9 14.7 %copy-start.2 = (f32[512,768]{1,0:T(8,128)S(1)}, f32[512,768]{1,0:T(8,128)}, u32[]{:S(2)}) copy-start(f32[512,768]{1,0:T(8,128)} %get-tuple-element.102) | copy-start | bytes 4718596
  696.9 40.6 %all-gather.25.cloned.1.call-start = ((), (), s32[]{:S(2)}) async-start(), calls=%async_computation.25 | async-start | bytes 2359296 | tf_op jit(solution)/shard_map/all_gather | solution.py:102
  711.5 9.5 copy-start.6
  723.5 66.3 %reduce-scatter.27.cloned.1.call-start = ((), (), s32[]{:S(2)}) async-start(), calls=%async_computation.26 | async-start | bytes 4718592 | tf_op jit(solution)/shard_map/reduce_scatter | solution.py:106
  742.4 124.6 %all-gather.27.cloned.1.call-start = ((), (), s32[]{:S(2)}) async-start(), calls=%async_computation.27 | async-start | bytes 2359296 | tf_op jit(solution)/shard_map/all_gather | solution.py:111
  804.0 9.2 copy-start.14
  836.2 63.7 %all-gather.29.cloned.1.call-start = ((), (), s32[]{:S(2)}) async-start(), calls=%async_computation.28 | async-start | bytes 2359296 | tf_op jit(solution)/shard_map/all_gather | solution.py:112
  860.7 101.5 %all-gather.17.cloned.1.call-start = ((), (), s32[]{:S(2)}) async-start(), calls=%async_computation.18 | async-start | bytes 6291456 | tf_op jit(solution)/shard_map/all_gather | solution.py:85
  861.3 38.6 %copy-start.17 = (bf16[768,2,2,192]{0,3,2,1:T(8,128)(2,1)S(1)}, bf16[768,2,2,192]{0,3,2,1:T(8,128)(2,1)}, u32[]{:S(2)}) copy-start(bf16[768,2,2,192]{0,3,2,1:T(8,128)(2,1)} %copy.50) | copy-start | bytes 3538948
  861.3 135.2 %reduce-scatter.29.cloned.1.call-start = ((), (), s32[]{:S(2)}) async-start(), calls=%async_computation.29 | async-start | bytes 4718592 | tf_op jit(solution)/shard_map/reduce_scatter | solution.py:122
  905.4 199.6 %reduce-scatter.21.cloned.1.call-start = ((), (), s32[]{:S(2)}) async-start(), calls=%async_computation.19 | async-start | bytes 4718592 | tf_op jit(solution)/shard_map/reduce_scatter | solution.py:93
  970.5 444.7 %all-reduce.7.cloned.1.call-start = ((), (), s32[]{:S(2)}) async-start(), calls=%async_computation.30 | async-start | bytes 25952256 | tf_op jit(solution)/shard_map/psum | solution.py:272
  971.9 7.5 copy-start.42
  971.9 7.5 copy-start.47
  996.5 108.5 %copy-start.7 = (bf16[512,768]{1,0:T(8,128)(2,1)S(1)}, bf16[512,768]{1,0:T(8,128)(2,1)}, u32[]{:S(2)}) copy-start(bf16[512,768]{1,0:T(8,128)(2,1)} %param.33) | copy-start | bytes 2359300
  996.5 108.5 %copy-start.40 = (f32[512]{0:T(512)S(1)}, f32[512]{0:T(512)}, u32[]{:S(2)}) copy-start(f32[512]{0:T(512)} %copy-done.39) | copy-start | bytes 6148
  1415.2 6.4 copy-start.15
  (40 other events, 107.0 us)
Sparse Core Ops, SparseCore 0:
  16.7 14.9 all-gather.10
  36.7 47.2 reduce-scatter.10
  87.0 46.8 reduce-scatter.12
  158.6 30.6 all-gather.12
  194.3 14.4 reduce-scatter.14
  210.4 13.8 all-gather.18
  226.7 13.8 all-gather.14
  243.1 103.1 reduce-scatter.22
  348.6 102.7 reduce-scatter.18
  453.8 102.7 reduce-scatter.16
  565.1 60.2 all-gather.20
  627.5 60.2 all-gather.22
  697.0 14.4 reduce-scatter.24
  723.6 13.8 all-gather.24
  742.5 47.2 reduce-scatter.26
  836.3 30.6 all-gather.26
  869.1 30.6 all-gather.28
  901.9 60.2 all-gather.16
  965.2 14.4 reduce-scatter.28
  982.6 14.9 reduce-scatter.20
  1001.8 413.3 all-reduce.6
where the time goes:
time: 1450 us; the launch traced here: 1440 us
  waiting for transfers between devices  1030 us (71%)
  matrix products  174 us (12%)
  blocking collectives  120 us (8%)
  other arithmetic  64.8 us (4%)
  local copies, waits for them, and re-layouts  31.5 us (2%)
  between operations  15 us (1%)
    psum x1, waiting for transfers between devices, per_device(): lax.psum(grad_w_key.astype(jnp.bfloat16), 'dp').astype(jnp.float32)  306 us
    reduce_scatter x2, waiting for transfers between devices, sum_heads(): lax.psum_scatter(first, 'col', scatter_dimension=1, tiled=True)  148 us
    reduce_scatter x2, waiting for transfers between devices, sum_heads(): lax.psum_scatter(second, 'col', scatter_dimension=1, tiled=True)  145 us
    reduce_scatter x2, waiting for transfers between devices, sum_heads_back(): return lax.psum_scatter(value, 'col', scatter_dimension=1, tiled=True)  135 us
    psum x1, blocking collectives, per_device(): lax.psum(gain_attn_rows.astype(jnp.bfloat16), 'dp').astype(jnp.float32)  96.2 us
    all_gather x2, waiting for transfers between devices, gather_heads(): return lax.all_gather(value, 'col', axis=1, tiled=True)  87.6 us
    all_gather x2, waiting for transfers between devices, gather_heads_back(): lax.all_gather(second, 'col', axis=1, tiled=True)  83 us
    all_gather x2, waiting for transfers between devices, gather_heads_back(): lax.all_gather(first, 'col', axis=1, tiled=True)  64.9 us
  transfers between devices with their start and end apart: 21, of which 19 were waited for; matrix products, arithmetic and copies ran while one was open for 9% of the time, Pallas kernels for 0%

commit v1 on v0

v1 whole, which is shorter than its diff:
```python
import functools
import math

import jax
import jax.numpy as jnp
from jax import lax
from jax.experimental import pallas as pl
from jax.experimental.pallas import tpu as pltpu
from jax.sharding import PartitionSpec as P

MESH = pl.DeviceIdType.MESH
BF16 = jnp.bfloat16
F32 = jnp.float32
TYPES = 6
LANE_DIMS = ("xa", "xb", "za", "zb")
ALL_DIMS = ("xa", "xb", "ya", "yb", "za", "zb")


class Place:
    def __init__(self):
        dp = lax.axis_index("dp")
        self.row = lax.axis_index("row")
        self.col = lax.axis_index("col")
        self.x = dp % 4
        self.yh = (dp // 4) % 2
        self.z = dp // 8
        y = self.yh * 2 + self.col
        self.bit = {
            "xa": ((self.x + 1) // 2) % 2,
            "xb": self.x // 2,
            "ya": ((y + 1) // 2) % 2,
            "yb": y // 2,
            "za": ((self.z + 1) // 2) % 2,
            "zb": self.z // 2,
        }

    def partner(self, dim):
        x, yh, z, row, col = self.x, self.yh, self.z, self.row, self.col
        if dim == "xa":
            x = x + 1 - 2 * (x % 2)
        elif dim == "xb":
            x = 3 - x
        elif dim == "za":
            z = z + 1 - 2 * (z % 2)
        elif dim == "zb":
            z = 3 - z
        elif dim in ("ya", "col"):
            col = 1 - col
        elif dim == "yb":
            col = 1 - col
            yh = 1 - yh
        elif dim == "y2":
            yh = 1 - yh
        elif dim == "row":
            row = 1 - row
        return ((z * 2 + yh) * 4 + x, row, col)


def greet(place, dims):
    barrier = pltpu.get_barrier_semaphore()
    for dim in dims:
        pl.semaphore_signal(barrier, inc=1, device_id=place.partner(dim), device_id_type=MESH)
    pl.semaphore_wait(barrier, len(dims))


def remote(place, dim, src, dst, send_sem, recv_sem):
    return pltpu.make_async_remote_copy(
        src_ref=src,
        dst_ref=dst,
        send_sem=send_sem,
        recv_sem=recv_sem,
        device_id=place.partner(dim),
        device_id_type=MESH,
    )


def exchange(value, dim, ident):
    def kernel(src, dst, send_sem, recv_sem):
        place = Place()
        greet(place, (dim,))
        copy = remote(place, dim, src, dst, send_sem, recv_sem)
        copy.start()
        copy.wait()

    return pl.pallas_call(
        kernel,
        out_shape=jax.ShapeDtypeStruct(value.shape, value.dtype),
        in_specs=[pl.BlockSpec(memory_space=pl.ANY)],
        out_specs=pl.BlockSpec(memory_space=pl.ANY),
        scratch_shapes=[pltpu.SemaphoreType.DMA, pltpu.SemaphoreType.DMA],
        compiler_params=pltpu.CompilerParams(collective_id=ident, has_side_effects=True),
        name="exchange_" + dim,
    )(value)


def span(kind, width, fixed):
    if kind == "tall":
        start, size = 0, width
        for bit in fixed:
            size //= 2
            start = start + bit * size
        return pl.ds(pl.multiple_of(start, 16) if fixed else 0, size), pl.ds(0, 128)
    rows, cols, row_start, col_start = 128, width, 0, 0
    for index, bit in enumerate(fixed):
        if index < 3:
            rows //= 2
            row_start = row_start + bit * rows
        else:
            cols //= 2
            col_start = col_start + bit * cols
    if len(fixed) > 0:
        row_start = pl.multiple_of(row_start, 16)
    if len(fixed) > 3:
        col_start = pl.multiple_of(col_start, 128)
    return pl.ds(row_start, rows), pl.ds(col_start, cols)


GATHER_ORDERS = (
    ("xa", "xb", "za", "zb"),
    ("xb", "xa", "zb", "za"),
    ("za", "zb", "xa", "xb"),
    ("zb", "za", "xb", "xa"),
)


class WeightGather:
    def __init__(self, place, kind, width, source, target, send_sem, recv_sem):
        self.place, self.kind, self.width = place, kind, width
        self.source, self.target = source, target
        self.send_sem, self.recv_sem = send_sem, recv_sem

    def part(self, ref, chunk, fixed, half=None):
        rows, cols = span(self.kind, self.width, fixed)
        base = 0 if half is None else half * 768
        if self.kind == "tall":
            return ref.at[rows, pl.ds(pl.multiple_of(base + chunk * 128, 128), 128)]
        return ref.at[pl.ds(pl.multiple_of(base + chunk * 128 + rows.start, 16), rows.size), cols]

    def copy(self, chunk, step):
        place = self.place
        me, other = place.col, 1 - place.col
        sems = (self.send_sem.at[chunk, step], self.recv_sem.at[chunk, step])
        if chunk >= 4:
            dim = "ya" if chunk == 4 else "yb"
            return remote(place, dim, self.part(self.source, chunk, ()), self.part(self.target, chunk, (), me), *sems)
        order = GATHER_ORDERS[chunk]
        bits = [place.bit[dim] for dim in reversed(order)]
        if step == 0:
            dim = "ya" if chunk < 2 else "yb"
            return remote(place, dim, self.part(self.source, chunk, bits), self.part(self.target, chunk, bits, me), *sems)
        bits = bits[: 5 - step]
        part = self.part(self.target, chunk, bits, other)
        return remote(place, order[step - 1], part, part, *sems)

    def begin(self, chunks):
        for chunk in chunks:
            self.copy(chunk, 0).start()

    def advance(self, step):
        for chunk in range(4):
            self.copy(chunk, step - 1).wait_recv()
            self.copy(chunk, step).start()

    def finish(self):
        for chunk in range(TYPES):
            self.copy(chunk, 4 if chunk < 4 else 0).wait_recv()

    def drain(self):
        for chunk in range(TYPES):
            for step in range(5 if chunk < 4 else 1):
                self.copy(chunk, step).wait_send()


def gather_weights(w_att, w_gate, w_up, w_down, tokens, gains, ident):
    kinds = (("wide", 2304), ("wide", 2048), ("wide", 2048), ("tall", 2048))

    def kernel(att, gate, up, down, tok, gain, att_out, gate_out, up_out, down_out, tok_out, gain_out,
               att_held, gate_held, up_held, down_held, send_sem, recv_sem, local_sem, small_send, small_recv):
        place = Place()
        greet(place, ALL_DIMS)
        sources = (att, gate, up, down)
        targets = (att_out, gate_out, up_out, down_out)
        held = (att_held, gate_held, up_held, down_held)
        small = [
            remote(place, "ya", tok.at[:, 1 - place.col], tok_out, small_send.at[0], small_recv.at[0]),
            remote(place, "ya", gain, gain_out, small_send.at[1], small_recv.at[1]),
        ]
        for copy in small:
            copy.start()
        jobs = [
            WeightGather(place, kind, width, source, target, send_sem.at[index], recv_sem.at[index])
            for index, ((kind, width), source, target) in enumerate(zip(kinds, sources, targets))
        ]
        for job in jobs:
            job.begin(range(4))
        for job in jobs:
            job.begin(range(4, 6))
        loads = [
            pltpu.make_async_copy(source, here, local_sem.at[0, index])
            for index, (source, here) in enumerate(zip(sources, held))
        ]
        half = pl.ds(pl.multiple_of(place.col * 768, 128), 768)
        stores = [
            pltpu.make_async_copy(
                here, target.at[:, half] if kind == "tall" else target.at[half], local_sem.at[1, index]
            )
            for index, ((kind, _), here, target) in enumerate(zip(kinds, held, targets))
        ]
        for copy in loads:
            copy.start()
        for load, store in zip(loads, stores):
            load.wait()
            store.start()
        for step in range(1, 5):
            for job in jobs:
                job.advance(step)
        for job in jobs:
            job.finish()
        for copy in stores:
            copy.wait()
        for copy in small:
            copy.wait()
        for job in jobs:
            job.drain()

    anywhere = pl.BlockSpec(memory_space=pl.ANY)
    return pl.pallas_call(
        kernel,
        out_shape=[
            jax.ShapeDtypeStruct((1536, 2304), BF16),
            jax.ShapeDtypeStruct((1536, 2048), BF16),
            jax.ShapeDtypeStruct((1536, 2048), BF16),
            jax.ShapeDtypeStruct((2048, 1536), BF16),
            jax.ShapeDtypeStruct((2, 256, 768), BF16),
            jax.ShapeDtypeStruct(gains.shape, F32),
        ],
        in_specs=[anywhere] * 6,
        out_specs=[anywhere] * 6,
        scratch_shapes=[
            pltpu.VMEM((768, 2304), BF16),
            pltpu.VMEM((768, 2048), BF16),
            pltpu.VMEM((768, 2048), BF16),
            pltpu.VMEM((2048, 768), BF16),
            pltpu.SemaphoreType.DMA((4, TYPES, 5)),
            pltpu.SemaphoreType.DMA((4, TYPES, 5)),
            pltpu.SemaphoreType.DMA((2, 4)),
            pltpu.SemaphoreType.DMA((2,)),
            pltpu.SemaphoreType.DMA((2,)),
        ],
        compiler_params=pltpu.CompilerParams(
            collective_id=ident, has_side_effects=True, vmem_limit_bytes=32 << 20
        ),
        name="gather_weights",
    )(w_att, w_gate, w_up, w_down, tokens, gains)


SUM_ORDERS = (
    ("xa", "xb", "ya", "yb", "za", "zb"),
    ("xb", "xa", "yb", "ya", "zb", "za"),
    ("ya", "yb", "za", "zb", "xa", "xb"),
    ("yb", "ya", "zb", "za", "xb", "xa"),
    ("za", "zb", "xa", "xb", "ya", "yb"),
    ("zb", "za", "xb", "xa", "yb", "ya"),
)
ALL_HALVES = pl.ds(0, 2)


class GradSum:
    def __init__(self, place, kind, width, first, held, landing, out, sems):
        self.place, self.kind, self.width = place, kind, width
        self.first, self.held, self.landing, self.out = first, held, landing, out
        self.send_sem, self.recv_sem, self.ag_send, self.ag_recv, self.own_sem = sems

    def view(self, ref, half, chunk, fixed):
        rows, cols = span(self.kind, self.width, fixed)
        return ref.at[half, chunk, rows, cols]

    def moves(self, chunk, step):
        place = self.place
        order = SUM_ORDERS[chunk]
        dim = order[step]
        regular = [d for d in order if d != "ya"]
        p, q, c = place.bit["ya"], place.bit["yb"], place.col
        y_at = [i for i, d in enumerate(order) if d[0] == "y"]
        a_first = order[y_at[0]] == "ya"
        own = [place.bit[d] for d in order[:step] if d != "ya"]
        flipped = [1 - bit for bit in own]
        if dim[0] != "y":
            bit = place.bit[dim]
            if step < y_at[0]:
                half_own = half_land = ALL_HALVES
            else:
                half_own = c
                half_land = c if a_first else 1 - c
            sent = [(half_own, own + [1 - bit])]
            lands = [(half_land, flipped + [1 - bit])]
            kept = [(half_own, own + [bit])]
            landed = [(half_land, flipped + [bit])]
            return dim, sent, lands, kept, landed
        if a_first and dim == "ya":
            sent = [(1 - p, own + [0]), (p, own + [1])]
            lands = [(1 - p, flipped + [0]), (p, flipped + [1])]
            kept = [(p, own + [0]), (1 - p, own + [1])]
            landed = [(p, flipped + [0]), (1 - p, flipped + [1])]
        elif a_first:
            send_half = (p + 1 - q) % 2
            sent = [(send_half, own + [1 - q])]
            lands = [(c, flipped + [1 - q])]
            kept = [(c, own + [q])]
            landed = [(1 - c, flipped + [q])]
        elif dim == "yb":
            sent = [(ALL_HALVES, own + [1 - q])]
            lands = [(ALL_HALVES, flipped + [1 - q])]
            kept = [(ALL_HALVES, own + [q])]
            landed = [(ALL_HALVES, flipped + [q])]
        else:
            sent = [(1 - c, own)]
            lands = [(1 - c, flipped)]
            kept = [(c, own)]
            landed = [(c, flipped)]
        return dim, sent, lands, kept, landed

    def sends(self, chunk, step):
        dim, sent, lands, _, _ = self.moves(chunk, step)
        source = self.first if step == 0 else self.held
        return [
            remote(
                self.place,
                dim,
                self.view(source, *region),
                self.view(self.landing, *there),
                self.send_sem.at[chunk, step, index],
                self.recv_sem.at[chunk, step, index],
            )
            for index, (region, there) in enumerate(zip(
                [(h, chunk, b) for h, b in sent], [(h, chunk, b) for h, b in lands]
            ))
        ]

    def start(self, step):
        for chunk in range(TYPES):
            for copy in self.sends(chunk, step):
                copy.start()

    def add(self, step):
        for chunk in range(TYPES):
            for copy in self.sends(chunk, step):
                copy.wait_recv()
            _, _, _, kept, landed = self.moves(chunk, step)
            for (half, bits), (from_half, from_bits) in zip(kept, landed):
                rows, cols = span(self.kind, self.width, bits)
                from_rows, from_cols = span(self.kind, self.width, from_bits)
                halves = 2 if half is ALL_HALVES else 1
                block = 16
                for h in range(halves):
                    here = h if halves == 2 else half
                    there = h if halves == 2 else from_half

                    def body(i, carry, here=here, there=there, rows=rows, cols=cols, from_rows=from_rows, from_cols=from_cols, chunk=chunk):
                        mine = (here, chunk, pl.ds(pl.multiple_of(rows.start + i * block, 16), block), cols)
                        came = (there, chunk, pl.ds(pl.multiple_of(from_rows.start + i * block, 16), block), from_cols)
                        self.held[mine] = self.held[mine] + self.landing[came]
                        return carry

                    lax.fori_loop(0, rows.size // block, body, 0)
            if step < 5:
                for copy in self.sends(chunk, step + 1):
                    copy.start()


    def spread(self, chunk, step):
        place = self.place
        order = SUM_ORDERS[chunk]
        stages = []
        for d in reversed(order):
            if d[0] == "y":
                if "y2" not in stages:
                    stages.append("y2")
            else:
                stages.append(d)
        dim = stages[step]
        keep = [d for d in order if d != "ya"]
        done = set(stages[:step])
        bits = [place.bit[d] for d in keep if ("y2" if d == "yb" else d) not in done]
        rows, cols = span(self.kind, self.width, bits)
        target = self.out.at[chunk, rows, cols]
        source = self.held.at[place.col, chunk, rows, cols] if step == 0 else target
        return remote(place, dim, source, target, self.ag_send.at[chunk, step], self.ag_recv.at[chunk, step])

    def own(self, chunk):
        place = self.place
        bits = [place.bit[d] for d in SUM_ORDERS[chunk] if d != "ya"]
        rows, cols = span(self.kind, self.width, bits)
        return pltpu.make_async_copy(
            self.held.at[place.col, chunk, rows, cols], self.out.at[chunk, rows, cols], self.own_sem.at[chunk]
        )

    def spread_start(self):
        for chunk in range(TYPES):
            self.spread(chunk, 0).start()
            self.own(chunk).start()

    def spread_next(self, step):
        for chunk in range(TYPES):
            if step == 1:
                self.own(chunk).wait()
            self.spread(chunk, step - 1).wait_recv()
            self.spread(chunk, step).start()

    def finish(self):
        for chunk in range(TYPES):
            self.spread(chunk, 4).wait_recv()

    def drain(self):
        for chunk in range(TYPES):
            for step in range(6):
                for copy in self.sends(chunk, step):
                    copy.wait_send()
            for step in range(5):
                self.spread(chunk, step).wait_send()


GROUPS = (("tall", 2048), ("wide", 2048), ("wide", 2048), ("wide", 2560))


def group_shape(kind, width):
    return (2048, 128) if kind == "tall" else (128, width)


def sum_gradients(parts, ident):
    count = len(GROUPS)

    def kernel(*refs):
        given, outs = refs[:count], refs[count : 2 * count]
        held, landing = refs[2 * count : 3 * count], refs[3 * count : 4 * count]
        send_sem, recv_sem, ag_send, ag_recv, own_sem, local_sem = refs[4 * count :]
        place = Place()
        greet(place, ALL_DIMS + ("y2",))
        jobs = [
            GradSum(
                place, kind, width, given[g], held[g], landing[g], outs[g],
                (send_sem.at[g], recv_sem.at[g], ag_send.at[g], ag_recv.at[g], own_sem.at[g]),
            )
            for g, (kind, width) in enumerate(GROUPS)
        ]
        loads = [pltpu.make_async_copy(given[g], held[g], local_sem.at[g]) for g in range(count)]
        for g in range(count):
            loads[g].start()
        jobs[0].start(0)
        jobs[1].start(0)
        steps = 6 + 6
        for wave in range(count + steps):
            if wave + 2 < count:
                jobs[wave + 2].start(0)
            for g in range(count):
                step = wave - g
                if step == 0:
                    loads[g].wait()
                if 0 <= step < 6:
                    jobs[g].add(step)
            for g in range(count):
                step = wave - g
                if step == 5:
                    jobs[g].spread_start()
                if 6 <= step < 10:
                    jobs[g].spread_next(step - 5)
                if step == 10:
                    jobs[g].finish()
        for job in jobs:
            job.drain()

    anywhere = pl.BlockSpec(memory_space=pl.ANY)
    shapes = [group_shape(*group) for group in GROUPS]
    return pl.pallas_call(
        kernel,
        out_shape=[jax.ShapeDtypeStruct((TYPES,) + shape, BF16) for shape in shapes],
        in_specs=[anywhere] * count,
        out_specs=[anywhere] * count,
        scratch_shapes=[pltpu.VMEM((2, TYPES) + shape, BF16) for shape in shapes] * 2
        + [
            pltpu.SemaphoreType.DMA((count, TYPES, 6, 2)),
            pltpu.SemaphoreType.DMA((count, TYPES, 6, 2)),
            pltpu.SemaphoreType.DMA((count, TYPES, 5)),
            pltpu.SemaphoreType.DMA((count, TYPES, 5)),
            pltpu.SemaphoreType.DMA((count, TYPES)),
            pltpu.SemaphoreType.DMA((count,)),
        ],
        compiler_params=pltpu.CompilerParams(
            collective_id=ident, has_side_effects=True, vmem_limit_bytes=60 << 20
        ),
        name="sum_gradients",
    )(*parts)


HEAD_DIM = 96
EPS = 1e-05
ROPE_BASE = 100000.0
NEG = -1e30


def matmul(left, right):
    return jnp.dot(left, right, preferred_element_type=F32)


def inner_left(left, right):
    return lax.dot_general(left, right, (((0,), (0,)), ((), ())), preferred_element_type=F32)


def inner_right(left, right):
    return lax.dot_general(left, right, (((1,), (1,)), ((), ())), preferred_element_type=F32)


def ordered(index, own, other, axis):
    return jnp.where(
        index == 0, jnp.concatenate([own, other], axis=axis), jnp.concatenate([other, own], axis=axis)
    )


def rotary(places):
    half = HEAD_DIM // 2
    rates = jnp.exp(-math.log(ROPE_BASE) * 2.0 * jnp.arange(half, dtype=F32) / HEAD_DIM)
    angle = places.astype(F32)[:, None] * rates[None, :]
    return (jnp.cos(angle)[:, None, :], jnp.sin(angle)[:, None, :])


def rotate(value, cosine, sine):
    half = value.shape[-1] // 2
    first, second = value[..., :half], value[..., half:]
    return jnp.concatenate([first * cosine - second * sine, second * cosine + first * sine], axis=-1)


def norm_forward(resid, gain):
    factor = lax.rsqrt(jnp.mean(resid * resid, axis=1, keepdims=True) + EPS)
    normed = resid * factor
    return normed, factor, (normed * gain).astype(BF16)


def norm_backward(grad_scaled, normed, factor, gain):
    grad_normed = grad_scaled * gain
    projection = jnp.mean(grad_normed * normed, axis=1, keepdims=True)
    return factor * (grad_normed - normed * projection), jnp.sum(grad_scaled * normed, axis=0)


def row_gather(value, row, ident):
    return ordered(row, value, exchange(value, "row", ident), 0)


def row_sum(value, row, ident):
    mine = lax.dynamic_slice_in_dim(value, row * 256, 256, 0)
    theirs = lax.dynamic_slice_in_dim(value, (1 - row) * 256, 256, 0)
    return mine + exchange(theirs, "row", ident)


SCALE = 1.0 / math.sqrt(HEAD_DIM)


def attention_blocks(col):
    return ((0, 512, col * 256), (256, 1024, 512 + col * 256))


def scores_of(piece, keys, start):
    raw = jnp.einsum("qkgd,tkd->kgqt", piece, keys, preferred_element_type=F32)
    reach = keys.shape[0]
    causal = jnp.arange(reach)[None, :] <= (start + jnp.arange(256))[:, None]
    return jnp.where(causal, raw * SCALE, NEG)


def attend(query, keys, values, col):
    outputs, logs = [], []
    for at, reach, start in attention_blocks(col):
        piece = query[at : at + 256].reshape(256, 4, 2, HEAD_DIM)
        scores = scores_of(piece, keys[:reach], start)
        top = jnp.max(scores, axis=-1, keepdims=True)
        powers = jnp.exp(scores - top)
        total = jnp.sum(powers, axis=-1, keepdims=True)
        shares = (powers / total).astype(BF16)
        mixed = jnp.einsum("kgqt,tkd->qkgd", shares, values[:reach], preferred_element_type=F32)
        outputs.append(mixed.reshape(256, 8 * HEAD_DIM))
        logs.append(top + jnp.log(total))
    return jnp.concatenate(outputs, axis=0), logs


def attend_back(query, keys, values, grad_out, logs, col):
    grad_queries = []
    grad_keys = jnp.zeros(keys.shape, F32)
    grad_values = jnp.zeros(values.shape, F32)
    for (at, reach, start), log in zip(attention_blocks(col), logs):
        piece = query[at : at + 256].reshape(256, 4, 2, HEAD_DIM)
        back = grad_out[at : at + 256].reshape(256, 4, 2, HEAD_DIM)
        shares = jnp.exp(scores_of(piece, keys[:reach], start) - log)
        grad_shares = jnp.einsum("qkgd,tkd->kgqt", back, values[:reach], preferred_element_type=F32)
        center = jnp.sum(grad_shares * shares, axis=-1, keepdims=True)
        grad_raw = (shares * (grad_shares - center) * SCALE).astype(BF16)
        grad_piece = jnp.einsum("kgqt,tkd->qkgd", grad_raw, keys[:reach], preferred_element_type=F32)
        grad_queries.append(grad_piece.reshape(256, 8, HEAD_DIM))
        grad_keys = grad_keys.at[:reach].add(
            jnp.einsum("kgqt,qkgd->tkd", grad_raw, piece, preferred_element_type=F32)
        )
        grad_values = grad_values.at[:reach].add(
            jnp.einsum("kgqt,qkgd->tkd", shares.astype(BF16), back, preferred_element_type=F32)
        )
    return jnp.concatenate(grad_queries, axis=0), grad_keys, grad_values


def per_device(
    hidden_in, gain_attn, w_query, w_key, w_value, w_out, gain_mlp, w_gate, w_up, w_down, out_grad
):
    row, col = lax.axis_index("row"), lax.axis_index("col")
    w_att = jnp.concatenate([w_query, w_key, w_value, w_out], axis=1)
    tokens = jnp.stack([hidden_in, out_grad]).reshape(2, 2, 256, 768)
    gains = jnp.zeros((8, 768), F32).at[0].set(gain_attn).at[1].set(gain_mlp)
    att, gate_w, up_w, down_w, token_part, gain_part = gather_weights(
        w_att, w_gate, w_up, w_down, tokens, gains, 1
    )
    q_w, k_w, v_w = att[:, :768], att[:, 768:1152], att[:, 1152:1536]
    out_w = jnp.concatenate([att[:768, 1536:], att[768:, 1536:]], axis=1)
    mine = lax.dynamic_index_in_dim(tokens, col, 1, False)
    both = ordered(col, mine, token_part, 2)
    gain_all = ordered(col, gains[:2], gain_part[:2], 1)
    gain_attn, gain_mlp = gain_all[0], gain_all[1]
    resid, og_own = both[0].astype(F32), both[1]

    normed_attn, factor_attn, scaled_attn = norm_forward(resid, gain_attn)
    s1 = row_gather(scaled_attn, row, 2)
    places = jnp.arange(512) // 256 * 512 + col * 256 + jnp.arange(512) % 256
    cosine, sine = rotary(places)
    query = rotate(matmul(s1, q_w).reshape(512, 8, HEAD_DIM), cosine, sine).astype(BF16)
    keys = rotate(matmul(s1, k_w).reshape(512, 4, HEAD_DIM), cosine, sine).astype(BF16)
    values = matmul(s1, v_w).astype(BF16)
    keyval = jnp.concatenate([keys.reshape(512, 384), values], axis=1)
    keyval = ordered(
        col, keyval.reshape(2, 256, 768), exchange(keyval, "col", 3).reshape(2, 256, 768), 1
    ).reshape(1024, 768)
    keys, values = keyval[:, :384].reshape(1024, 4, HEAD_DIM), keyval[:, 384:].reshape(1024, 4, HEAD_DIM)
    attended, logs = attend(query, keys, values, col)
    attended = attended.astype(BF16)
    middle = resid + row_sum(matmul(attended, out_w), row, 4)
    normed_mlp, factor_mlp, scaled_mlp = norm_forward(middle, gain_mlp)
    s2 = row_gather(scaled_mlp, row, 2)
    gate, upper = matmul(s2, gate_w), matmul(s2, up_w)
    logistic = jax.nn.sigmoid(gate)
    activated = gate * logistic
    hidden = (activated * upper).astype(BF16)
    block_out = (middle + row_sum(matmul(hidden, down_w), row, 4)).astype(BF16)

    og = row_gather(og_own, row, 2)
    part_down = jnp.einsum("tf,tcd->cfd", hidden, og.reshape(512, 12, 128), preferred_element_type=F32)
    grad_hidden = inner_right(og, down_w)
    grad_gate = (grad_hidden * upper * logistic * (1.0 + gate * (1.0 - logistic))).astype(BF16)
    grad_upper = (grad_hidden * activated).astype(BF16)
    part_gate, part_up = inner_left(s2, grad_gate), inner_left(s2, grad_upper)
    grad_scaled_mlp = row_sum(inner_right(grad_gate, gate_w) + inner_right(grad_upper, up_w), row, 4)
    grad_norm, gain_mlp_part = norm_backward(grad_scaled_mlp, normed_mlp, factor_mlp, gain_mlp)
    grad_middle = og_own.astype(F32) + grad_norm
    gm = row_gather(grad_middle.astype(BF16), row, 2)
    part_out = inner_left(attended, gm)
    grad_attended = inner_right(gm, out_w).astype(BF16)
    grad_query, grad_keys, grad_values = attend_back(query, keys, values, grad_attended, logs, col)
    grad_kv = jnp.concatenate([grad_keys.reshape(1024, 384), grad_values.reshape(1024, 384)], axis=1)
    grad_kv = grad_kv.reshape(2, 2, 256, 768)
    kv_mine = lax.dynamic_index_in_dim(grad_kv, col, 1, False)
    kv_theirs = lax.dynamic_index_in_dim(grad_kv, 1 - col, 1, False).astype(BF16)
    grad_kv = (kv_mine + exchange(kv_theirs, "col", 5).astype(F32)).reshape(512, 768)
    grad_query = rotate(grad_query, cosine, -sine).reshape(512, 768).astype(BF16)
    grad_keys = rotate(grad_kv[:, :384].reshape(512, 4, HEAD_DIM), cosine, -sine).reshape(512, 384).astype(BF16)
    grad_values = grad_kv[:, 384:].astype(BF16)
    grad_qkv = jnp.concatenate([grad_query, grad_keys, grad_values], axis=1)
    part_qkv = inner_left(s1, grad_qkv)
    grad_scaled_attn = row_sum(inner_right(grad_qkv, att[:, :1536]), row, 4)
    grad_norm, gain_attn_part = norm_backward(grad_scaled_attn, normed_attn, factor_attn, gain_attn)
    in_grad = (grad_middle + grad_norm).astype(BF16)

    gain_parts = jnp.stack([gain_attn_part, gain_mlp_part])
    gain_parts = gain_parts + exchange(jnp.pad(gain_parts, ((0, 6), (0, 0))), "row", 6)[:2]
    gain_rows = gain_parts.reshape(2, 2, 6, 128).transpose(1, 2, 0, 3).reshape(2, 6, 1, 256)
    part_att = jnp.concatenate(
        [
            part_qkv.astype(BF16).reshape(2, 6, 128, 1536),
            part_out.astype(BF16).reshape(6, 128, 2, 768).transpose(2, 0, 1, 3),
            jnp.pad(gain_rows.astype(BF16), ((0, 0), (0, 0), (0, 127), (0, 0))),
        ],
        axis=3,
    )
    sum_down, sum_gate, sum_up, sum_att = sum_gradients(
        (
            part_down.astype(BF16).reshape(2, 6, 2048, 128),
            part_gate.astype(BF16).reshape(2, 6, 128, 2048),
            part_up.astype(BF16).reshape(2, 6, 128, 2048),
            part_att,
        ),
        7,
    )
    results = jnp.stack([block_out, in_grad]).reshape(2, 256, 2, 768)
    own = lax.dynamic_index_in_dim(results, col, 2, False)
    other = exchange(lax.dynamic_index_in_dim(results, 1 - col, 2, False), "col", 8)
    results = ordered(col, own, other, 1)
    att_rows = sum_att.reshape(768, 2560).astype(F32)
    gain_sums = sum_att[:, 0, 2304:].astype(F32)
    return (
        results[0],
        results[1],
        gain_sums[:, :128].reshape(768),
        att_rows[:, :768],
        att_rows[:, 768:1152],
        att_rows[:, 1152:1536],
        att_rows[:, 1536:2304],
        gain_sums[:, 128:].reshape(768),
        sum_gate.reshape(768, 2048).astype(F32),
        sum_up.reshape(768, 2048).astype(F32),
        sum_down.transpose(1, 0, 2).reshape(2048, 768).astype(F32),
    )


def solution(mesh):
    tokens, weight_in, weight_out, gain = P(("dp", "row"), "col"), P("col", "row"), P("row", "col"), P("col")
    return jax.shard_map(
        per_device,
        mesh=mesh,
        in_specs=(
            tokens, gain, weight_in, weight_in, weight_in, weight_out, gain, weight_in, weight_in, weight_out, tokens,
        ),
        out_specs=(
            tokens, tokens, gain, weight_in, weight_in, weight_in, weight_out, gain, weight_in, weight_in, weight_out,
        ),
        check_vma=False,
    )
```

time: 1450 us -> 703 us (0.48)
  waiting for transfers between devices: 1030 us -> 0 us
  Pallas kernels: 0 us -> 344 us
  blocking collectives: 120 us -> 0 us
  local copies, waits for them, and re-layouts: 31.5 us -> 109 us
    reduce_scatter x10 -> x0, waiting for transfers between devices: 456 us -> none  [the longest x2 148 us: sum_heads(): lax.psum_scatter(first, 'col', scatter_dimension=1, tiled=True)]
    pallas_call x0 -> x14, Pallas kernels: none -> 344 us  [the longest x1 179 us: sum_gradients(): pl.pallas_call(kernel, out_shape=[jax.ShapeDtypeStruct((TYPES,) + shape,...]
    psum x1 -> x0, waiting for transfers between devices: 306 us -> none  [per_device(): lax.psum(grad_w_key.astype(jnp.bfloat16), 'dp').astype(jnp.float32)]
    all_gather x10 -> x0, waiting for transfers between devices: 268 us -> none  [the longest x2 87.6 us: gather_heads(): return lax.all_gather(value, 'col', axis=1, tiled=True)]
    psum x6 -> x0, blocking collectives: 120 us -> none  [the longest x1 96.2 us: per_device(): lax.psum(gain_attn_rows.astype(jnp.bfloat16), 'dp').astype(jnp.float32)]
    convert_element_type x0 -> x8, local copies, waits for them, and re-layouts: none -> 17 us  [the longest x1 8.61 us: per_device(): part_down.astype(BF16).reshape(2, 6, 2048, 128)]
    unnamed x106 -> x151, local copies, waits for them, and re-layouts: 16.8 us -> 30.8 us
    dot_general x6 -> x5, matrix products: 40.6 us -> 30.3 us  [inner_right(): lax.dot_general(left, right, (((1,), (1,)), ((), ())), preferred_element_...]
  transfers between devices with their start and end apart: 21 -> 0, of which waited for: 19 -> 0; matrix products, arithmetic and copies ran while one was open for 9% -> 0% of each run, Pallas kernels for 0% -> 0%
where the time goes in v1:
time: 703 us; the launch traced here: 696 us
  Pallas kernels  344 us (49%)
  matrix products  172 us (24%)
  local copies, waits for them, and re-layouts  109 us (16%)
  other arithmetic  68.5 us (10%)
    pallas_call x1, Pallas kernels, sum_gradients(): pl.pallas_call(kernel, out_shape=[jax.ShapeDtypeStruct((TYPES,) + shape,...  179 us
    pallas_call x12, Pallas kernels, exchange(): pl.pallas_call(kernel, out_shape=jax.ShapeDtypeStruct(value.shape, value....  87.4 us
    pallas_call x1, Pallas kernels, gather_weights(): pl.pallas_call(kernel, out_shape=[jax.ShapeDtypeStruct((1536, 2304), BF16...  78.1 us
    dot_general x7, matrix products, matmul(): return jnp.dot(left, right, preferred_element_type=F32)  34.7 us
    unnamed x151, local copies, waits for them, and re-layouts  30.8 us
    dot_general x5, matrix products, inner_right(): lax.dot_general(left, right, (((1,), (1,)), ((), ())), preferred_element_...  30.3 us
    dot_general x2, matrix products, attend_back(): jnp.einsum('kgqt,tkd->qkgd', grad_raw, keys[:reach], preferred_element_ty...  23.7 us
    dot_general x2, matrix products, attend_back(): jnp.einsum('kgqt,qkgd->tkd', grad_raw, piece, preferred_element_type=F32)  22.7 us

profile of v1, /device:TPU:0, one launch (start us, length us, event | category | flops | bytes accessed | tf_op | source)
XLA Modules:
  0.0 695.7 jit_solution(4991242783152415032)
XLA Ops:
  9.3 78.1 %gather_weights.1 = (bf16[1536,2304]{1,0:T(8,128)(2,1)}, bf16[1536,2048]{1,0:T(8,128)(2,1)S(1)}, bf16[1536,2048]{1,0:T(8,128)(2,1)}, bf16[2048,1536]{1,0:T(8,128...) custom-call(bf16[768,2304]{1,0:T(8,128)(2,1)S(1)} %pad_maximum_fusion.att, bf16[768,2048]{1,0:T(8,128)(2,1)S(1)} %copy-done, ...), custom_call_target="tpu_custom_call" | custom-call | tf_op jit(solution)/shard_map/gather_weights/pallas_call | solution.py:227
  94.6 3.9 fusion.76
  105.6 19.9 %exchange_col.3 = bf16[512,768]{1,0:T(8,128)(2,1)} custom-call(bf16[512,768]{1,0:T(8,128)(2,1)} %pad_maximum_fusion.9.src), custom_call_target="tpu_custom_call" | custom-call | tf_op jit(solution)/shard_map/exchange_col/pallas_call | solution.py:85
  132.4 4.1 fusion.28
  156.2 5.1 fusion.73
  181.8 9.2 %fusion.111 = f32[512,2048]{1,0:T(8,128)} fusion(bf16[1536,2048]{1,0:T(8,128)(2,1)} %get-tuple-element.113, bf16[256,1536]{1,0:T(8,128)(2,1)} %exchange_row.11, bf16[256,1536]{1,0:T(8,128)(2,1)} %multiply_convert_fusion.3.src, pred[]{:T(512)S(6)} %eq.7), kind=kOutput, calls=%fused_computation.222 | convolution fusion | flops 3228303360 | bytes 12058625 | tf_op jit(solution)/shard_map/dot_general | solution.py:502
  191.1 4.9 fusion.112
  200.0 12.3 %multiply_convert_fusion = (bf16[512,2048]{1,0:T(8,128)(2,1)S(1)}, bf16[512,2048]{1,0:T(8,128)(2,1)S(1)}, bf16[512,2048]{1,0:T(8,128)(2,1)}) fusion(f32[512,2048]{1,0:T(8,128)} %fusion.112, f32[512,2048]{1,0:T(8,128)} %fusion.111, bf16[2048,1536]{1,0:T(8,128)(2,1)} %get-tuple-element.114, bf16[256,1536]{1,0:T(8,128)(2,1)} %exchange_row.13, ...), kind=kOutput, calls=%fused_computation.32 | convolution fusion | flops 3244032000 | bytes 22544384 | tf_op jit(solution)/shard_map/dot_general | solution.py:510
  215.8 5.8 convolution_add_fusion
  236.7 4.0 fusion.68
  246.8 8.7 %fusion.36 = f32[4,96,2,256]{3,1,2,0:T(8,128)} fusion(bf16[512,4,96,1]{0,2,3,1:T(8,128)(2,1)} %bitcast.266, f32[4,512,256,2]{2,1,3,0:T(8,128)} %fusion.124, f32[4,2,256,512]{2,3,1,0:T(8,128)} %copy-done.10, f32[4,2,256]{2,1,0:T(2,128)} %bitcast.285), kind=kOutput, calls=%fused_computation.71 | convolution fusion | flops 208669184 | bytes 9576448 | tf_op jit(solution)/shard_map/kgqt,tkd->qkgd/dot_general | solution.py:594
  258.0 5.7 fusion.125
  263.7 15.0 %fusion.23 = f32[4,96,2,256]{3,1,2,0:T(8,128)} fusion(bf16[1024,4,96,1]{0,2,3,1:T(8,128)(2,1)} %bitcast.244, f32[4,1024,256,2]{2,1,3,0:T(8,128)} %fusion.125, f32[4,2,256,1024]{2,3,1,0:T(8,128)} %copy-done.4, f32[4,2,256]{2,1,0:T(2,128)S(1)} %bitcast.282), kind=kOutput, calls=%fused_computation.54 | convolution fusion | flops 417336320 | bytes 18358272 | tf_op jit(solution)/shard_map/kgqt,tkd->qkgd/dot_general | solution.py:594
  284.9 6.0 bitcast_add_fusion
  298.2 8.7 %fusion.72 = f32[512,4,96]{0,2,1:T(8,128)} fusion(bf16[256,4,2,96]{0,3,2,1:T(8,128)(2,1)} %bitcast.265, f32[4,512,256,2]{2,1,3,0:T(8,128)} %fusion.124, f32[4,2,256,512]{2,3,1,0:T(8,128)} %copy-done.10, f32[4,2,256]{2,1,0:T(2,128)} %bitcast.286), kind=kOutput, calls=%fused_computation.127 | convolution fusion | flops 208669184 | bytes 9576448 | tf_op jit(solution)/shard_map/kgqt,qkgd->tkd/dot_general | solution.py:597
  306.9 13.9 %bitcast_add_fusion.1 = f32[1024,4,96]{0,2,1:T(8,128)} fusion(f32[512,4,96]{0,2,1:T(8,128)} %fusion.72, bf16[256,4,2,96]{0,3,2,1:T(8,128)(2,1)S(1)} %bitcast.262, f32[4,1024,256,2]{2,1,3,0:T(8,128)} %fusion.125, f32[4,2,256,1024]{2,3,1,0:T(8,128)} %copy-done.4, f32[4,2,256]{2,1,0:T(2,128)S(1)} %bitcast.284), kind=kOutput, calls=%fused_computation.112 | convolution fusion | flops 417729536 | bytes 19537920 | tf_op jit(solution)/shard_map/kgqt,qkgd->tkd/dot_general | solution.py:597
  330.2 19.9 %exchange_col.4 = bf16[2,256,768]{2,1,0:T(8,128)(2,1)} custom-call(bf16[2,256,768]{2,1,0:T(8,128)(2,1)} %fusion.79.src), custom_call_target="tpu_custom_call" | custom-call | tf_op jit(solution)/shard_map/exchange_col/pallas_call | solution.py:85
  360.5 7.3 %convolution_convert_fusion = bf16[1536,1536]{1,0:T(8,128)(2,1)} fusion(bf16[512,384]{0,1:T(8,128)(2,1)} %copy.104, bf16[512,384]{0,1:T(8,128)(2,1)} %bitcast.278, bf16[512,768]{0,1:T(8,128)(2,1)} %bitcast.271, bf16[256,1536]{1,0:T(8,128)(2,1)} %exchange_row.9, bf16[256,1536]{1,0:T(8,128)(2,1)} %fusion.38.src, pred[]{:T(512)S(6)} %eq.7), kind=kOutput, calls=%fused_computation.14 | convolution fusion | flops 2430074880 | bytes 7864321 | tf_op jit(solution)/shard_map/dot_general | solution.py:506
  370.7 6.4 reshape.519
  380.6 4.7 fusion.9
  385.4 6.7 fusion.122
  405.3 7.2 %fusion.6.refs_3_ = bf16[2,6,128,2560]{3,2,1,0:T(8,128)(2,1)} fusion(bf16[2,6,1,256]{3,2,1,0:T(2,128)(2,1)S(1)} %reshape.537, bf16[2,6,128,768]{3,2,1,0:T(8,128)(2,1)} %bitcast.240, bf16[2,6,128,1536]{3,2,1,0:T(8,128)(2,1)} %bitcast.249), kind=kLoop, calls=%fused_computation.13 | loop fusion | flops 31457280 | bytes 14948352 | tf_op jit(solution)/shard_map/concatenate | solution.py:676
  412.5 5.5 convolution_convert_fusion.1
  418.1 5.6 convolution_convert_fusion.2
  428.2 8.7 %convert_bitcast_fusion.1 = bf16[12,2048,128]{1,2,0:T(8,128)(2,1)} fusion(bf16[512,2048]{1,0:T(8,128)(2,1)} %get-tuple-element.142, bf16[256,12,128]{0,2,1:T(8,128)(2,1)} %bitcast.273, bf16[256,12,128]{0,2,1:T(8,128)(2,1)} %bitcast.274, pred[]{:T(512)S(6)} %eq.7), kind=kOutput, calls=%fused_computation.20 | convolution fusion | flops 3231449088 | bytes 9961473 | tf_op jit(solution)/shard_map/tf,tcd->cfd/dot_general | solution.py:647
  436.9 8.6 %copy.77 = bf16[12,2048,128]{2,1,0:T(8,128)(2,1)} copy(bf16[12,2048,128]{1,2,0:T(8,128)(2,1)} %convert_bitcast_fusion.1) | data formatting | bytes 12582912 | tf_op jit(solution)/shard_map/convert_element_type | solution.py:686
  445.5 178.8 %sum_gradients.1 = (bf16[6,2048,128]{2,1,0:T(8,128)(2,1)}, bf16[6,128,2048]{2,1,0:T(8,128)(2,1)}, bf16[6,128,2048]{2,1,0:T(8,128)(2,1)}, bf16[6,128,2560]{2,1,0:T(8,128)(2,1)}) custom-call(bf16[2,6,2048,128]{3,2,1,0:T(8,128)(2,1)} %bitcast.237, bf16[2,6,128,2048]{3,2,1,0:T(8,128)(2,1)} %bitcast.242, bf16[2,6,128,2048]{3,2,1,0:T(8,128)(2,1)} %bitcast.241, ...), custom_call_target="tpu_custom_call" | custom-call | tf_op jit(solution)/shard_map/sum_gradients/pallas_call | solution.py:474
  624.3 5.0 convert_bitcast_fusion
  629.3 6.6 copy.81
  635.9 6.7 copy.82
  663.9 4.8 fusion.43
  672.4 19.9 %exchange_col.5 = bf16[2,256,768]{2,1,0:T(8,128)(2,1)} custom-call(bf16[2,256,768]{2,1,0:T(8,128)(2,1)} %get-tuple-element.158.src), custom_call_target="tpu_custom_call" | custom-call | tf_op jit(solution)/shard_map/exchange_col/pallas_call | solution.py:85
  (263 shorter events, 185.5 us)
Async XLA Ops:
  90.5 83.8 %copy-start.5 = (bf16[2,256,1536]{2,1,0:T(8,128)(2,1)}, bf16[2,256,1536]{2,1,0:T(8,128)(2,1)S(1)}, u32[]{:S(2)}) copy-start(bf16[2,256,1536]{2,1,0:T(8,128)(2,1)S(1)} %maximum_select_fusion) | copy-start | bytes 4718596
  90.7 7.8 %copy-start.54 = (f32[256]{0:T(256)}, f32[256]{0:T(256)S(1)}, u32[]{:S(2)}) copy-start(f32[256]{0:T(256)S(1)} %add_rsqrt_fusion.1) | copy-start | bytes 3076
  90.8 7.7 %copy-start.45 = (f32[1536]{0:T(1024)}, f32[1536]{0:T(1024)S(1)}, u32[]{:S(2)}) copy-start(f32[1536]{0:T(1024)S(1)} %get-tuple-element.135) | copy-start | bytes 18436
  99.7 36.9 %copy-start.30 = (f32[512,48]{0,1:T(8,128)}, f32[512,48]{0,1:T(8,128)S(1)}, u32[]{:S(2)}) copy-start(f32[512,48]{0,1:T(8,128)S(1)} %get-tuple-element.177) | copy-start | bytes 294916
  136.9 14.2 %copy-start.28 = (bf16[256,8,96]{0,2,1:T(8,128)(2,1)}, bf16[256,8,96]{0,2,1:T(8,128)(2,1)S(1)}, u32[]{:S(2)}) copy-start(bf16[256,8,96]{0,2,1:T(8,128)(2,1)S(1)} %get-tuple-element.172) | copy-start | bytes 1179652
  155.9 5.5 copy-start.51
  156.2 5.2 copy-start.16
  161.3 6.5 copy-start.62
  176.5 55.0 %copy-start.52 = (f32[256]{0:T(256)}, f32[256]{0:T(256)S(1)}, u32[]{:S(2)}) copy-start(f32[256]{0:T(256)S(1)} %add_rsqrt_fusion) | copy-start | bytes 3076
  177.6 13.5 %slice-start = ((s8[6291456]{0:T(1024)(128)(4,1)}), s8[2097152]{0:T(1024)(128)(4,1)S(1)}, s32[]{:S(2)}) async-start(s8[6291456]{0:T(1024)(128)(4,1)} %bitcast.232), calls=%async_computation | async-start | bytes 4194304
  181.8 9.3 %slice-start.1 = ((s8[6291456]{0:T(1024)(128)(4,1)}), s8[4194304]{0:T(1024)(128)(4,1)S(1)}, s32[]{:S(2)}) async-start(s8[6291456]{0:T(1024)(128)(4,1)} %bitcast.232), calls=%async_computation.1 | async-start | bytes 8388608
  181.8 9.3 %copy-start.20 = (bf16[256,1536]{1,0:T(8,128)(2,1)S(1)}, bf16[256,1536]{1,0:T(8,128)(2,1)}, u32[]{:S(2)}) copy-start(bf16[256,1536]{1,0:T(8,128)(2,1)} %multiply_convert_fusion.3.src) | copy-start | bytes 2359300
  181.8 9.3 %copy-start.38 = (bf16[256,1536]{1,0:T(8,128)(2,1)S(1)}, bf16[256,1536]{1,0:T(8,128)(2,1)}, u32[]{:S(2)}) copy-start(bf16[256,1536]{1,0:T(8,128)(2,1)} %exchange_row.11) | copy-start | bytes 2359300
  196.1 16.2 %slice-start.2 = ((s8[6291456]{0:T(1024)(128)(4,1)}), s8[2097152]{0:T(1024)(128)(4,1)S(1)}, s32[]{:S(2)}) async-start(s8[6291456]{0:T(1024)(128)(4,1)} %bitcast.234), calls=%async_computation.2 | async-start | bytes 4194304
  200.0 12.4 %slice-start.3 = ((s8[6291456]{0:T(1024)(128)(4,1)}), s8[4194304]{0:T(1024)(128)(4,1)S(1)}, s32[]{:S(2)}) async-start(s8[6291456]{0:T(1024)(128)(4,1)} %bitcast.234), calls=%async_computation.3 | async-start | bytes 8388608
  231.5 5.2 copy-start.56
  242.8 12.6 %copy-start.14 = (bf16[256,768]{0,1:T(8,128)(2,1)}, bf16[256,768]{0,1:T(8,128)(2,1)S(1)}, u32[]{:S(2)}) copy-start(bf16[256,768]{0,1:T(8,128)(2,1)S(1)} %copy.61) | copy-start | bytes 1179652
  258.0 5.7 copy-start.47
  298.2 8.7 %copy-start.29 = (bf16[256,8,96]{0,2,1:T(8,128)(2,1)S(1)}, bf16[256,8,96]{0,2,1:T(8,128)(2,1)}, u32[]{:S(2)}) copy-start(bf16[256,8,96]{0,2,1:T(8,128)(2,1)} %copy-done.28) | copy-start | bytes 1179652
  350.2 6.2 copy-start.31
  350.2 6.2 copy-start.37
  360.5 7.3 %copy-start.27 = (bf16[256,1536]{1,0:T(8,128)(2,1)S(1)}, bf16[256,1536]{1,0:T(8,128)(2,1)}, u32[]{:S(2)}) copy-start(bf16[256,1536]{1,0:T(8,128)(2,1)} %fusion.110.src) | copy-start | bytes 2359300
  360.5 7.4 %copy-start.40 = (bf16[256,1536]{1,0:T(8,128)(2,1)S(1)}, bf16[256,1536]{1,0:T(8,128)(2,1)}, u32[]{:S(2)}) copy-start(bf16[256,1536]{1,0:T(8,128)(2,1)} %exchange_row.15) | copy-start | bytes 2359300
  360.5 7.4 %copy-start.61 = (bf16[4,96,2,256]{3,1,2,0:T(8,128)(2,1)S(1)}, bf16[4,96,2,256]{3,1,2,0:T(8,128)(2,1)}, u32[]{:S(2)}) copy-start(bf16[4,96,2,256]{3,1,2,0:T(8,128)(2,1)} %fusion.74) | copy-start | bytes 1179652
  360.5 7.4 %copy-start.63 = (bf16[4,96,2,256]{3,1,2,0:T(8,128)(2,1)S(1)}, bf16[4,96,2,256]{3,1,2,0:T(8,128)(2,1)}, u32[]{:S(2)}) copy-start(bf16[4,96,2,256]{3,1,2,0:T(8,128)(2,1)} %copy-done.62) | copy-start | bytes 1179652
  385.4 6.7 copy-start.25
  405.3 7.2 %copy-start.21 = (bf16[256,1536]{1,0:T(8,128)(2,1)S(1)}, bf16[256,1536]{1,0:T(8,128)(2,1)}, u32[]{:S(2)}) copy-start(bf16[256,1536]{1,0:T(8,128)(2,1)} %multiply_convert_fusion.3.src) | copy-start | bytes 2359300
  405.3 7.2 %copy-start.39 = (bf16[256,1536]{1,0:T(8,128)(2,1)S(1)}, bf16[256,1536]{1,0:T(8,128)(2,1)}, u32[]{:S(2)}) copy-start(bf16[256,1536]{1,0:T(8,128)(2,1)} %exchange_row.11) | copy-start | bytes 2359300
  405.3 7.2 %copy-start.66 = (bf16[512,2048]{1,0:T(8,128)(2,1)S(1)}, bf16[512,2048]{1,0:T(8,128)(2,1)}, u32[]{:S(2)}) copy-start(bf16[512,2048]{1,0:T(8,128)(2,1)} %copy-done.65) | copy-start | bytes 6291460
  412.5 5.5 copy-start.68
  658.7 5.1 copy-start.53
  658.7 5.1 copy-start.57
  (41 other events, 112.6 us)
